TPU v7x, 32 devices: a whole 2x2x4 slice. The times are simulated.
32 devices in a mesh: vir: 8 (over z, y), occ: 4 (over x, core).
Axes of the slice: x: 2, y: 2, z: 4, core: 2. Of those that a mesh axis runs over, the one named last changes fastest.
Arguments:
- tiles: float32 [4096, 128, 128], P('vir'), may hold values from -0.02734375 to 0.02734375
- tile_slot: int32 [4096], P('vir'), may hold values from 0 to 2048, as said below
- amplitudes: float32 [262144, 1024], P('vir', 'occ'), may hold values from -6 to 6
- occ_energy: float32 [32], replicated, may hold values from -2 to -0.5
- vir_energy: float32 [32], replicated, may hold values from 0.5 to 3
Outputs:
- update: float32 [1024, 1024], P('vir', 'occ')
Inputs may be any that keep to these rules, and one draw needn't show every extreme that they name: `tile_slot`: for each index v of vir, the slots v * 512 to v * 512 + 511 name distinct block positions below 2048, live slots first, then the empty value 8 * 256; each index has 128 or more live slots and some index has all 512 live.
All inputs are finite; a program needn't handle non-finite values.
Results may differ from a plain program's by a relative error of at most 0.0003.
Values sent between devices are 32-bit elements; how exact they have to be, the bound alone decides.
A program may use at most 320 MiB of HBM per device.

v0:
```python
import jax
import jax.numpy as jnp
from jax import lax
from jax.sharding import PartitionSpec as P

NO = 32
NW = 32


def per_device(tiles, tile_slot, amplitudes, occ_energy, vir_energy):
    highest = lax.Precision.HIGHEST
    slot_count = tiles.shape[0]
    tile_size = tiles.shape[1]
    cd_dev, ij_dev = amplitudes.shape
    col_blocks = cd_dev // tile_size
    pair_rows = NW * NW
    row_blocks = pair_rows // tile_size
    occ_local = ij_dev // NO
    own_rows = pair_rows // lax.axis_size("vir")
    flat_index = lax.broadcasted_iota(jnp.int32, (row_blocks * col_blocks, slot_count), 0)
    placing = (flat_index == tile_slot[None, :]).astype(jnp.float32)
    blocks = jnp.dot(placing, tiles.reshape(slot_count, tile_size * tile_size), precision=highest)
    dense_block = blocks.reshape(row_blocks, col_blocks, tile_size, tile_size)
    dense_block = dense_block.transpose(0, 2, 1, 3).reshape(row_blocks * tile_size, cd_dev)
    partial_sum = jnp.dot(dense_block, amplitudes, precision=highest)
    swapped = partial_sum.reshape(NW, NW, ij_dev).transpose(1, 0, 2).reshape(pair_rows, ij_dev)
    moved = lax.all_to_all(
        swapped.reshape(pair_rows, occ_local, NO), "occ", split_axis=2, concat_axis=1, tiled=True
    )
    numerator = partial_sum + moved.transpose(0, 2, 1).reshape(pair_rows, ij_dev)
    total = lax.psum_scatter(numerator, "vir", scatter_dimension=0, tiled=True)
    row_ids = lax.axis_index("vir") * own_rows + lax.broadcasted_iota(jnp.int32, (own_rows,), 0)
    first_orb = row_ids // NW
    second_orb = row_ids % NW
    orbital = lax.broadcasted_iota(jnp.int32, (NW,), 0)
    energy_first = jnp.sum(
        jnp.where(first_orb[:, None] == orbital[None, :], vir_energy[None, :], 0.0), axis=1
    )
    energy_second = jnp.sum(
        jnp.where(second_orb[:, None] == orbital[None, :], vir_energy[None, :], 0.0), axis=1
    )
    own_occ = lax.dynamic_slice_in_dim(occ_energy, lax.axis_index("occ") * occ_local, occ_local)
    denominator = (
        own_occ[None, :, None]
        + occ_energy[None, None, :]
        - energy_first[:, None, None]
        - energy_second[:, None, None]
    )
    return (total.reshape(own_rows, occ_local, NO) / denominator).reshape(own_rows, ij_dev)


def solution(mesh):
    in_specs = (P("vir", None, None), P("vir"), P("vir", "occ"), P(), P())
    out_specs = P("vir", "occ")
    return jax.shard_map(
        per_device, mesh=mesh, in_specs=in_specs, out_specs=out_specs, check_vma=False
    )
```

profile of v0, /device:TPU:0, one launch (start us, length us, event | category | flops | bytes accessed | tf_op | source)
XLA Modules:
  0.0 440.2 jit_solution(16350599682012340363)
XLA Ops:
  6.5 0.0 reduce-scatter.2.cloned.1.call-start
  6.5 32.9 %copy.37 = f32[64,8,128,128]{3,1,2,0:T(8,128)} copy(f32[64,8,128,128]{3,2,1,0:T(8,128)} %bitcast.40) | data formatting | bytes 67108864
  39.5 0.0 copy-start
  39.5 33.5 %copy.20 = f32[16384,512]{1,0:T(8,128)} copy(f32[16384,512]{0,1:T(8,128)} %bitcast.39) | data formatting | bytes 67108864 | tf_op jit(solution)/shard_map/dot_general | solution.py:22
  72.9 0.0 copy-done
  72.9 0.7 fusion.13
  73.7 114.9 %fusion.3 = f32[8,256,128,128]{3,1,2,0:T(8,128)} fusion(f32[128,128,512,1]{2,1,0,3:T(8,128)} %bitcast.41, pred[8,256,512,1]{2,1,3,0:T(32,128)(4,1)S(1)} %fusion.13), kind=kOutput, calls=%fused_computation.4 | convolution fusion | flops 206158430208 | bytes 168820736 | tf_op jit(solution)/shard_map/dot_general | solution.py:22
  188.5 0.0 copy-start.1
  188.6 0.0 copy-start.2
  188.6 151.4 %fusion = f32[1024,256]{1,0:T(8,128)S(1)} fusion(f32[32768,256]{1,0:T(8,128)} %param.7, f32[128,8,256,128]{3,2,1,0:T(8,128)} %bitcast.20), kind=kOutput, calls=%fused_computation | convolution fusion | flops 103079215104 | bytes 168820736 | tf_op jit(solution)/shard_map/dot_general | solution.py:25
  339.9 0.6 copy.38
  340.5 2.4 reshape_reshape.3
  343.0 3.2 copy.22
  346.2 18.5 %all_to_all.18 = f32[1024,8,32]{0,1,2:T(8,128)S(1)} all-to-all(f32[1024,8,32]{0,1,2:T(8,128)S(1)} %copy.22), channel_id=1, replica_groups=mesh['vir'=8,'occ'=4] {'occ'}, dimensions={2} | all-to-all | bytes 2097152 | tf_op jit(solution)/shard_map/all_to_all | solution.py:27
  364.7 0.6 copy.24
  365.3 0.6 copy.25
  365.9 0.3 copy.26
  366.2 1.1 add.62
  367.4 0.0 reduce-scatter.2.cloned.1.call-update
  367.4 0.0 copy-done.1
  367.4 0.1 dynamic_slice.3
  367.5 0.1 broadcast_reduce_fusion
  367.6 0.1 add.65
  367.7 0.1 add.67
  367.8 0.0 copy-done.2
  367.8 0.1 select_reduce_fusion.1
  367.9 63.8 %reduce-scatter.2.cloned.1.call-done = f32[128,256]{1,0:T(8,128)} async-done(((f32[1024,256]{1,0:T(8,128)}), f32[128,256]{1,0:T(8,128)}) %reduce-scatter.2.cloned.1.call-update) | async-done | bytes 131088 | tf_op jit(solution)/shard_map/reduce_scatter | solution.py:31
  431.7 1.7 subtract_divide_fusion
  (4 shorter events, 0.0 us)
Async XLA Ops:
  6.5 425.2 %reduce-scatter.2.cloned.1.call-start = ((), (), s32[]{:S(2)}) async-start(), calls=%async_computation.2 | async-start | bytes 1179648 | tf_op jit(solution)/shard_map/reduce_scatter | solution.py:31
  39.5 33.5 %copy-start = (s32[512]{0:T(512)S(1)}, s32[512]{0:T(512)}, u32[]{:S(2)}) copy-start(s32[512]{0:T(512)} %param.6) | copy-start | bytes 6148
  188.5 178.9 %copy-start.1 = (f32[32]{0:T(128)S(1)}, f32[32]{0:T(128)}, u32[]{:S(2)}) copy-start(f32[32]{0:T(128)} %param.8) | copy-start | bytes 388
  188.6 179.2 %copy-start.2 = (f32[32]{0:T(128)S(1)}, f32[32]{0:T(128)}, u32[]{:S(2)}) copy-start(f32[32]{0:T(128)} %param.9) | copy-start | bytes 388
Sparse Core Ops, SparseCore 0:
  367.5 64.1 reduce-scatter.1
where the time goes:
time: 441 us; the launch traced here: 440 us
  matrix products  266 us (60%)
  local copies, waits for them, and re-layouts  74.6 us (17%)
  waiting for transfers between devices  63.9 us (14%)
  blocking collectives  18.5 us (4%)
  between operations  13.5 us (3%)
    dot_general x1, matrix products, per_device(): partial_sum = jnp.dot(dense_block, amplitudes, precision=highest)  151 us
    dot_general x1, matrix products, per_device(): jnp.dot(placing, tiles.reshape(slot_count, tile_size * tile_size), precis...  115 us
    reduce_scatter x1, waiting for transfers between devices, per_device(): total = lax.psum_scatter(numerator, 'vir', scatter_dimension=0, tiled=True)  63.8 us
    dot_general x1, local copies, waits for them, and re-layouts, per_device(): jnp.dot(placing, tiles.reshape(slot_count, tile_size * tile_size), precis...  33.5 us
    unnamed x7, local copies, waits for them, and re-layouts  32.9 us
    all_to_all x1, blocking collectives, per_device(): lax.all_to_all(swapped.reshape(pair_rows, occ_local, NO), 'occ', split_ax...  18.5 us
  transfers between devices with their start and end apart: 1, of which 1 were waited for; matrix products, arithmetic and copies ran while one was open for 0% of the time, Pallas kernels for 0%

commit v1 on v0

--- a/solution.py
+++ b/solution.py
@@ -1,28 +1,193 @@
+import functools
+
 import jax
 import jax.numpy as jnp
 from jax import lax
+from jax.experimental import pallas as pl
+from jax.experimental.pallas import tpu as pltpu
 from jax.sharding import PartitionSpec as P
 
 NO = 32
 NW = 32
+GROUP = 4
+UNROLL = 4
+TILE_DEPTH = 4
+AMP_DEPTH = 6
+MIB = 1024 * 1024
+
+
+def split_two(x):
+    high = x.astype(jnp.bfloat16)
+    low = (x - high.astype(jnp.float32)).astype(jnp.bfloat16)
+    return high, low
+
+
+def ladder_kernel(
+    row_blocks, slots_ref, slot_vec_ref, tiles_hbm, amp_hbm, out_ref,
+    amp_high, amp_low, stage, ring, place_slot, place_col, group_row, cursor,
+    amp_sem, ring_sem,
+):
+    slot_count, tile, _ = tiles_hbm.shape
+    cd, width = amp_hbm.shape
+    col_blocks = cd // tile
+    chunk = stage.shape[1]
+    chunks = cd // chunk
+    per_chunk = slot_count // chunks
+    batch = GROUP * UNROLL
+
+    def amp_copy(i):
+        slot = lax.rem(i, AMP_DEPTH)
+        return pltpu.make_async_copy(
+            amp_hbm.at[pl.ds(pl.multiple_of(i * chunk, chunk), chunk)],
+            stage.at[slot], amp_sem.at[slot],
+        )
+
+    for i in range(min(AMP_DEPTH - 1, chunks)):
+        amp_copy(i).start()
+
+    slot_vec = slot_vec_ref[...]
+    start = jnp.int32(0)
+    for r in range(row_blocks):
+        inside = (slot_vec >= r * col_blocks) & (slot_vec < (r + 1) * col_blocks)
+        count = jnp.sum(jnp.where(inside, 1.0, 0.0)).astype(jnp.int32)
+        cursor[r] = start
+        start = start + ((count + GROUP - 1) // GROUP) * GROUP
+        for t in range(1, GROUP):
+            at = jnp.maximum(start - t, 0)
+            place_slot[at] = 0
+            place_col[at] = col_blocks
+    total = start
+    for t in range(batch):
+        place_slot[total + t] = 0
+        place_col[total + t] = col_blocks
+    for t in range(UNROLL):
+        group_row[total // GROUP + t] = 0
+    cursor[row_blocks] = total + batch
+    steps = (total + batch - 1) // batch
+
+    out_ref[...] = jnp.zeros_like(out_ref)
+    amp_high[pl.ds(cd, tile), :] = jnp.zeros((tile, width), jnp.bfloat16)
+    amp_low[pl.ds(cd, tile), :] = jnp.zeros((tile, width), jnp.bfloat16)
+
+    def load_chunk(i, carry):
+        amp_copy(i).wait()
+
+        @pl.when(i + AMP_DEPTH - 1 < chunks)
+        def _():
+            amp_copy(i + AMP_DEPTH - 1).start()
+
+        high, low = split_two(stage[lax.rem(i, AMP_DEPTH)])
+        rows = pl.ds(pl.multiple_of(i * chunk, chunk), chunk)
+        amp_high[rows, :] = high
+        amp_low[rows, :] = low
+        for q in range(per_chunk):
+            k = i * per_chunk + q
+            s = slots_ref[k]
+            r = lax.div(s, jnp.int32(col_blocks))
+            at = cursor[r]
+            place_slot[at] = k
+            place_col[at] = s - r * col_blocks
+            group_row[at // GROUP] = r
+            cursor[r] = at + 1
+        return carry
+
+    lax.fori_loop(0, chunks, load_chunk, 0)
+
+    def start_tiles(i):
+        slot = lax.rem(i, TILE_DEPTH)
+        for t in range(batch):
+            pltpu.make_async_copy(
+                tiles_hbm.at[place_slot[i * batch + t]],
+                ring.at[slot, t], ring_sem.at[slot],
+            ).start()
+
+    def wait_tiles(i):
+        slot = lax.rem(i, TILE_DEPTH)
+        pltpu.make_async_copy(
+            tiles_hbm.at[pl.ds(0, batch)], ring.at[slot], ring_sem.at[slot]
+        ).wait()
+
+    for i in range(TILE_DEPTH - 1):
+        @pl.when(i < steps)
+        def _(i=i):
+            start_tiles(jnp.int32(i))
+
+    def multiply(i, carry):
+        wait_tiles(i)
+
+        @pl.when(i + TILE_DEPTH - 1 < steps)
+        def _():
+            start_tiles(i + TILE_DEPTH - 1)
+
+        slot = lax.rem(i, TILE_DEPTH)
+        products = []
+        for u in range(UNROLL):
+            highs, lows, amp_highs, amp_lows = [], [], [], []
+            for t in range(GROUP):
+                at = u * GROUP + t
+                high, low = split_two(ring[slot, at])
+                first = pl.multiple_of(place_col[i * batch + at] * tile, tile)
+                highs.append(high)
+                lows.append(low)
+                amp_highs.append(amp_high[pl.ds(first, tile), :])
+                amp_lows.append(amp_low[pl.ds(first, tile), :])
+            left = jnp.concatenate(highs + lows + highs, axis=1)
+            right = jnp.concatenate(amp_highs + amp_highs + amp_lows, axis=0)
+            products.append(jnp.dot(left, right, preferred_element_type=jnp.float32))
+        for u in range(UNROLL):
+            first = pl.multiple_of(group_row[i * UNROLL + u] * tile, tile)
+            out_ref[pl.ds(first, tile), :] += products[u]
+        return carry
+
+    lax.fori_loop(0, steps, multiply, 0)
+
+
+def ladder_partial(tiles, tile_slot, amplitudes, row_blocks):
+    slot_count, tile, _ = tiles.shape
+    cd, width = amplitudes.shape
+    chunk = min(512, cd)
+    batch = GROUP * UNROLL
+    lanes = min(128, slot_count)
+    places = 2 * slot_count + row_blocks * GROUP + 2 * batch
+    flops = 6 * slot_count * tile * tile * width
+    return pl.pallas_call(
+        functools.partial(ladder_kernel, row_blocks),
+        out_shape=jax.ShapeDtypeStruct((row_blocks * tile, width), jnp.float32),
+        in_specs=[
+            pl.BlockSpec(memory_space=pltpu.SMEM),
+            pl.BlockSpec(memory_space=pltpu.VMEM),
+            pl.BlockSpec(memory_space=pl.ANY),
+            pl.BlockSpec(memory_space=pl.ANY),
+        ],
+        out_specs=pl.BlockSpec(memory_space=pltpu.VMEM),
+        scratch_shapes=[
+            pltpu.VMEM((cd + tile, width), jnp.bfloat16),
+            pltpu.VMEM((cd + tile, width), jnp.bfloat16),
+            pltpu.VMEM((AMP_DEPTH, chunk, width), jnp.float32),
+            pltpu.VMEM((TILE_DEPTH, batch, tile, tile), jnp.float32),
+            pltpu.SMEM((places,), jnp.int32),
+            pltpu.SMEM((places,), jnp.int32),
+            pltpu.SMEM((places,), jnp.int32),
+            pltpu.SMEM((row_blocks + 1,), jnp.int32),
+            pltpu.SemaphoreType.DMA((AMP_DEPTH,)),
+            pltpu.SemaphoreType.DMA((TILE_DEPTH,)),
+        ],
+        compiler_params=pltpu.CompilerParams(vmem_limit_bytes=56 * MIB),
+        cost_estimate=pl.CostEstimate(
+            flops=flops,
+            bytes_accessed=4 * (tiles.size + amplitudes.size),
+            transcendentals=0,
+        ),
+    )(tile_slot, tile_slot.reshape(slot_count // lanes, lanes), tiles, amplitudes)
 
 
 def per_device(tiles, tile_slot, amplitudes, occ_energy, vir_energy):
-    highest = lax.Precision.HIGHEST
-    slot_count = tiles.shape[0]
-    tile_size = tiles.shape[1]
-    cd_dev, ij_dev = amplitudes.shape
-    col_blocks = cd_dev // tile_size
+    ij_dev = amplitudes.shape[1]
     pair_rows = NW * NW
-    row_blocks = pair_rows // tile_size
+    row_blocks = pair_rows // tiles.shape[1]
     occ_local = ij_dev // NO
     own_rows = pair_rows // lax.axis_size("vir")
-    flat_index = lax.broadcasted_iota(jnp.int32, (row_blocks * col_blocks, slot_count), 0)
-    placing = (flat_index == tile_slot[None, :]).astype(jnp.float32)
-    blocks = jnp.dot(placing, tiles.reshape(slot_count, tile_size * tile_size), precision=highest)
-    dense_block = blocks.reshape(row_blocks, col_blocks, tile_size, tile_size)
-    dense_block = dense_block.transpose(0, 2, 1, 3).reshape(row_blocks * tile_size, cd_dev)
-    partial_sum = jnp.dot(dense_block, amplitudes, precision=highest)
+    partial_sum = ladder_partial(tiles, tile_slot, amplitudes, row_blocks)
     swapped = partial_sum.reshape(NW, NW, ij_dev).transpose(1, 0, 2).reshape(pair_rows, ij_dev)
     moved = lax.all_to_all(
         swapped.reshape(pair_rows, occ_local, NO), "occ", split_axis=2, concat_axis=1, tiled=True

time: 441 us -> 150 us (0.34)
  matrix products: 266 us -> 0 us
  local copies, waits for them, and re-layouts: 74.6 us -> 9.38 us
  Pallas kernels: 0 us -> 28.3 us
  waiting for transfers between devices: 63.9 us -> 75.3 us
    dot_general x2 -> x0, matrix products: 266 us -> none  [the longest x1 151 us: per_device(): partial_sum = jnp.dot(dense_block, amplitudes, precision=highest)]
    dot_general x1 -> x0, local copies, waits for them, and re-layouts: 33.5 us -> none  [per_device(): jnp.dot(placing, tiles.reshape(slot_count, tile_size * tile_size), precis...]
    unnamed x7 -> x4, local copies, waits for them, and re-layouts: 32.9 us -> 0.01 us
    pallas_call x0 -> x1, Pallas kernels: none -> 28.3 us  [ladder_partial(): pl.pallas_call(functools.partial(ladder_kernel, row_blocks), out_shape=ja...]
    reduce_scatter x1, waiting for transfers between devices: 63.8 us -> 75.3 us  [per_device(): total = lax.psum_scatter(numerator, 'vir', scatter_dimension=0, tiled=True)]
where the time goes in v1:
time: 150 us; the launch traced here: 149 us
  waiting for transfers between devices  75.3 us (50%)
  Pallas kernels  28.3 us (19%)
  blocking collectives  18.5 us (12%)
  between operations  13.5 us (9%)
  local copies, waits for them, and re-layouts  9.38 us (6%)
  other arithmetic  4.11 us (3%)
    reduce_scatter x1, waiting for transfers between devices, per_device(): total = lax.psum_scatter(numerator, 'vir', scatter_dimension=0, tiled=True)  75.3 us
    pallas_call x1, Pallas kernels, ladder_partial(): pl.pallas_call(functools.partial(ladder_kernel, row_blocks), out_shape=ja...  28.3 us
    all_to_all x1, blocking collectives, per_device(): lax.all_to_all(swapped.reshape(pair_rows, occ_local, NO), 'occ', split_ax...  18.5 us
    another operation x2, local copies, waits for them, and re-layouts, per_device(): swapped.reshape(pair_rows, occ_local, NO)  5.65 us
  transfers between devices with their start and end apart: 1, of which 1 were waited for; matrix products, arithmetic and copies ran while one was open for 0% of the time, Pallas kernels for 0%

profile of v1, /device:TPU:0, one launch (start us, length us, event | category | flops | bytes accessed | tf_op | source)
XLA Modules:
  0.0 149.0 jit_solution(2130972966716596891)
XLA Ops:
  6.5 0.0 reduce-scatter.2.cloned.1.call-start
  6.5 0.0 copy-start
  6.5 0.0 copy-start.1
  6.5 28.3 %shard_map.55 = f32[1024,256]{1,0:T(8,128)} custom-call(s32[512]{0:T(512)} %slots_ref.1, s32[4,128]{1,0:T(4,128)} %bitcast.17, f32[512,128,128]{2,1,0:T(8,128)} %tiles_hbm.1, f32[32768,256]{1,0:T(8,128)} %amp_hbm.1), custom_call_target="tpu_custom_call" | custom-call | flops 12884901888 | bytes 67108864 | tf_op jit(solution)/shard_map/pallas_call | solution.py:153
  34.8 1.8 %copy.25 = f32[32,32,256]{2,0,1:T(8,128)S(1)} copy(f32[32,32,256]{2,1,0:T(8,128)} %bitcast.12) | data formatting | bytes 2097152 | tf_op jit(solution)/shard_map/reshape | solution.py:191
  36.7 2.4 %reshape_reshape.3 = f32[1024,8,32]{2,1,0:T(8,128)} reshape(f32[32,32,256]{2,1,0:T(8,128)S(1)} %bitcast.13) | data formatting | bytes 2097152 | tf_op jit(solution)/shard_map/reshape;reshape | solution.py:193
  39.1 3.2 %copy.18 = f32[1024,8,32]{0,1,2:T(8,128)S(1)} copy(f32[1024,8,32]{2,1,0:T(8,128)} %reshape_reshape.3) | data formatting | bytes 2097152 | tf_op jit(solution)/shard_map/reshape;reshape | solution.py:193
  42.3 18.5 %all_to_all.18 = f32[1024,8,32]{0,1,2:T(8,128)S(1)} all-to-all(f32[1024,8,32]{0,1,2:T(8,128)S(1)} %copy.18), channel_id=1, replica_groups=mesh['vir'=8,'occ'=4] {'occ'}, dimensions={2} | all-to-all | bytes 2097152 | tf_op jit(solution)/shard_map/all_to_all | solution.py:192
  60.8 0.6 copy.20
  61.4 0.6 copy.21
  62.0 0.3 copy.22
  62.4 2.3 %add.58 = f32[1024,256]{1,0:T(8,128)} add(f32[1024,256]{1,0:T(8,128)} %shard_map.55, f32[1024,256]{1,0:T(8,128)S(1)} %copy.22) | non-fusion elementwise | flops 262144 | bytes 3145728 | tf_op jit(solution)/shard_map/add | solution.py:195
  64.7 0.0 reduce-scatter.2.cloned.1.call-update
  64.7 0.0 copy-done
  64.7 0.1 dynamic_slice.3
  64.8 0.1 broadcast_reduce_fusion
  64.9 0.1 add.61
  65.0 0.1 add.63
  65.1 0.0 copy-done.1
  65.1 0.1 select_reduce_fusion.1
  65.2 75.3 %reduce-scatter.2.cloned.1.call-done = f32[128,256]{1,0:T(8,128)} async-done(((f32[1024,256]{1,0:T(8,128)}), f32[128,256]{1,0:T(8,128)}) %reduce-scatter.2.cloned.1.call-update) | async-done | bytes 131088 | tf_op jit(solution)/shard_map/reduce_scatter | solution.py:196
  140.5 1.7 %subtract_divide_fusion = f32[128,256]{1,0:T(8,128)} fusion(f32[128,256]{1,0:T(8,128)} %reduce-scatter.2.cloned.1.call-done, f32[128]{0:T(128)S(1)} %get-tuple-element.6, f32[128]{0:T(128)S(1)} %get-tuple-element.5, f32[256]{0:T(256)S(1)} %add.64), kind=kLoop, calls=%fused_computation.1 | loop fusion | flops 98304 | bytes 264192 | tf_op jit(solution)/shard_map/div | solution.py:214
  (3 shorter events, 0.0 us)
Async XLA Ops:
  6.5 133.9 %reduce-scatter.2.cloned.1.call-start = ((), (), s32[]{:S(2)}) async-start(), calls=%async_computation.2 | async-start | bytes 1179648 | tf_op jit(solution)/shard_map/reduce_scatter | solution.py:196
  6.5 58.2 %copy-start = (f32[32]{0:T(128)S(1)}, f32[32]{0:T(128)}, u32[]{:S(2)}) copy-start(f32[32]{0:T(128)} %param.8) | copy-start | bytes 388
  6.5 58.6 %copy-start.1 = (f32[32]{0:T(128)S(1)}, f32[32]{0:T(128)}, u32[]{:S(2)}) copy-start(f32[32]{0:T(128)} %param.9) | copy-start | bytes 388
Sparse Core Ops, SparseCore 0:
  64.9 75.5 reduce-scatter.1

commit v2 on v1

v2 whole, which is shorter than its diff:
```python
import functools

import jax
import jax.numpy as jnp
from jax import lax
from jax.experimental import pallas as pl
from jax.experimental.pallas import tpu as pltpu
from jax.sharding import PartitionSpec as P

NO = 32
NW = 32
GROUP = 4
UNROLL = 4
TILE_DEPTH = 5
AMP_PARTS = 8
MIB = 1024 * 1024


def split_two(x):
    high = x.astype(jnp.bfloat16)
    low = (x - high.astype(jnp.float32)).astype(jnp.bfloat16)
    return high, low


def ladder_kernel(
    row_blocks, slots_ref, slot_vec_ref, tiles_hbm, amp_hbm, out_ref,
    amp, ring, place_slot, place_col, group_row, cursor, amp_sem, ring_sem,
):
    slot_count, tile, _ = tiles_hbm.shape
    cd, width = amp_hbm.shape
    col_blocks = cd // tile
    batch = GROUP * UNROLL
    part = cd // AMP_PARTS

    def amp_copy(i):
        rows = pl.ds(i * part, part)
        return pltpu.make_async_copy(amp_hbm.at[rows], amp.at[rows], amp_sem.at[i])

    for i in range(AMP_PARTS):
        amp_copy(i).start()

    slot_vec = slot_vec_ref[...]
    start = jnp.int32(0)
    for r in range(row_blocks):
        inside = (slot_vec >= r * col_blocks) & (slot_vec < (r + 1) * col_blocks)
        count = jnp.sum(jnp.where(inside, 1.0, 0.0)).astype(jnp.int32)
        cursor[r] = start
        start = start + ((count + GROUP - 1) // GROUP) * GROUP
        for t in range(1, GROUP):
            at = jnp.maximum(start - t, 0)
            place_slot[at] = 0
            place_col[at] = col_blocks
    total = start
    for t in range(batch):
        place_slot[total + t] = 0
        place_col[total + t] = col_blocks
    for t in range(UNROLL):
        group_row[total // GROUP + t] = 0
    cursor[row_blocks] = total + batch
    steps = (total + batch - 1) // batch

    out_ref[...] = jnp.zeros_like(out_ref)
    amp[pl.ds(cd, tile), :] = jnp.zeros((tile, width), jnp.float32)

    def place(i, carry):
        for q in range(8):
            k = i * 8 + q
            s = slots_ref[k]
            r = lax.div(s, jnp.int32(col_blocks))
            at = cursor[r]
            place_slot[at] = k
            place_col[at] = s - r * col_blocks
            group_row[at // GROUP] = r
            cursor[r] = at + 1
        return carry

    lax.fori_loop(0, slot_count // 8, place, 0)

    def start_tiles(i):
        slot = lax.rem(i, TILE_DEPTH)
        for t in range(batch):
            pltpu.make_async_copy(
                tiles_hbm.at[place_slot[i * batch + t]],
                ring.at[slot, t], ring_sem.at[slot],
            ).start()

    def wait_tiles(i):
        slot = lax.rem(i, TILE_DEPTH)
        pltpu.make_async_copy(
            tiles_hbm.at[pl.ds(0, batch)], ring.at[slot], ring_sem.at[slot]
        ).wait()

    for i in range(TILE_DEPTH - 1):
        @pl.when(i < steps)
        def _(i=i):
            start_tiles(jnp.int32(i))
    for i in range(AMP_PARTS):
        amp_copy(i).wait()

    def multiply(i, carry):
        wait_tiles(i)

        @pl.when(i + TILE_DEPTH - 1 < steps)
        def _():
            start_tiles(i + TILE_DEPTH - 1)

        slot = lax.rem(i, TILE_DEPTH)
        products = []
        for u in range(UNROLL):
            highs, lows, amp_highs, amp_lows = [], [], [], []
            for t in range(GROUP):
                at = u * GROUP + t
                high, low = split_two(ring[slot, at])
                first = pl.multiple_of(place_col[i * batch + at] * tile, tile)
                amp_high, amp_low = split_two(amp[pl.ds(first, tile), :])
                highs.append(high)
                lows.append(low)
                amp_highs.append(amp_high)
                amp_lows.append(amp_low)
            left = jnp.concatenate(highs + lows + highs, axis=1)
            right = jnp.concatenate(amp_highs + amp_highs + amp_lows, axis=0)
            products.append(jnp.dot(left, right, preferred_element_type=jnp.float32))
        for u in range(UNROLL):
            first = pl.multiple_of(group_row[i * UNROLL + u] * tile, tile)
            out_ref[pl.ds(first, tile), :] += products[u]
        return carry

    lax.fori_loop(0, steps, multiply, 0)


def ladder_partial(tiles, tile_slot, amplitudes, row_blocks):
    slot_count, tile, _ = tiles.shape
    cd, width = amplitudes.shape
    batch = GROUP * UNROLL
    lanes = min(128, slot_count)
    places = 2 * slot_count + row_blocks * GROUP + 2 * batch
    flops = 6 * slot_count * tile * tile * width
    return pl.pallas_call(
        functools.partial(ladder_kernel, row_blocks),
        out_shape=jax.ShapeDtypeStruct((row_blocks * tile, width), jnp.float32),
        in_specs=[
            pl.BlockSpec(memory_space=pltpu.SMEM),
            pl.BlockSpec(memory_space=pltpu.VMEM),
            pl.BlockSpec(memory_space=pl.ANY),
            pl.BlockSpec(memory_space=pl.ANY),
        ],
        out_specs=pl.BlockSpec(memory_space=pltpu.VMEM),
        scratch_shapes=[
            pltpu.VMEM((cd + tile, width), jnp.float32),
            pltpu.VMEM((TILE_DEPTH, batch, tile, tile), jnp.float32),
            pltpu.SMEM((places,), jnp.int32),
            pltpu.SMEM((places,), jnp.int32),
            pltpu.SMEM((places,), jnp.int32),
            pltpu.SMEM((row_blocks + 1,), jnp.int32),
            pltpu.SemaphoreType.DMA((AMP_PARTS,)),
            pltpu.SemaphoreType.DMA((TILE_DEPTH,)),
        ],
        compiler_params=pltpu.CompilerParams(vmem_limit_bytes=56 * MIB),
        cost_estimate=pl.CostEstimate(
            flops=flops,
            bytes_accessed=4 * (tiles.size + amplitudes.size),
            transcendentals=0,
        ),
    )(tile_slot, tile_slot.reshape(slot_count // lanes, lanes), tiles, amplitudes)


def one_hot(shape, want):
    row = lax.broadcasted_iota(jnp.int32, shape, 0)
    col = lax.broadcasted_iota(jnp.int32, shape, 1)
    return jnp.where(want(row, col), 1.0, 0.0)


def mirror_fits(vir_size, occ_size):
    if vir_size % 2 or NW % vir_size or NO % occ_size:
        return False
    a_own, i_own = NW // vir_size, NO // occ_size
    if 128 % (i_own * i_own) or a_own * a_own * i_own * i_own != 1024:
        return False
    return a_own % (128 // (i_own * i_own)) == 0


def exchange_kernel(
    vir_size, occ_size, partial_ref, out_ref,
    pair_in, line_out, line_in, outgoing, incoming,
    rows_out, cols_out, rows_in, cols_in,
    pair_send, pair_recv, line_send, line_recv, mirror_send, mirror_recv,
):
    exact = lax.Precision.HIGHEST
    own_rows, width = out_ref.shape
    a_own, i_own = NW // vir_size, NO // occ_size
    folds = 128 // (i_own * i_own)
    a_fold = a_own // folds
    devices = vir_size * occ_size
    line = vir_size // 2
    vir = lax.axis_index("vir")
    occ = lax.axis_index("occ")
    me = vir * occ_size + occ
    z, y = vir // 2, vir % 2

    barrier = pltpu.get_barrier_semaphore()

    def greet(k, carry):
        other = (me + k) % devices
        pl.semaphore_signal(
            barrier, inc=1,
            device_id={"vir": other // occ_size, "occ": other % occ_size},
            device_id_type=pl.DeviceIdType.MESH,
        )
        return carry

    lax.fori_loop(1, devices, greet, 0)
    pl.semaphore_wait(barrier, devices - 1)

    def block(z_to, y_to):
        first = (z_to * 2 + y_to) * own_rows
        return pl.ds(pl.multiple_of(first, own_rows), own_rows)

    middle = line // 2
    order = sorted(range(1, line), key=lambda s: abs(s - middle)) + [0]
    pair_copies = {}
    for s in order:
        pair_copies[s] = pltpu.make_async_remote_copy(
            src_ref=partial_ref.at[block((z + s) % line, 1 - y)],
            dst_ref=pair_in.at[s],
            send_sem=pair_send.at[s], recv_sem=pair_recv.at[s],
            device_id={"vir": z * 2 + 1 - y, "occ": occ},
            device_id_type=pl.DeviceIdType.MESH,
        )
        pair_copies[s].start()

    half = vir_size * a_fold * a_own
    lanes = occ_size * 128
    square = i_own * i_own

    def place_rows(at, r):
        fold, rest = at // half, at % half
        v, p, b = rest // (a_fold * a_own), (rest // a_own) % a_fold, rest % a_own
        return r == (fold * a_fold + p) * NW + v * a_own + b

    def return_rows(r, at):
        fold, rest = at // half, at % half
        v, p, b = rest // (a_fold * a_own), (rest // a_own) % a_fold, rest % a_own
        return r == b * NW + v * a_own + fold * a_fold + p

    rows_out[...] = one_hot((own_rows, own_rows), place_rows)
    rows_in[...] = one_hot((own_rows, own_rows), return_rows)
    for fold in range(folds):
        def place_cols(c, at):
            o, rest = at // 128, at % 128
            j, i = (rest % square) // i_own, rest % i_own
            return (rest // square == fold) & (c == i * NO + o * i_own + j)

        def return_cols(at, c):
            o, rest = at // 128, at % 128
            j, i = (rest % square) // i_own, rest % i_own
            return (rest // square == fold) & (c == j * NO + o * i_own + i)

        cols_out[fold] = one_hot((width, lanes), place_cols)
        cols_in[fold] = one_hot((lanes, width), return_cols)

    line_copies = {}
    for s in order:
        pair_copies[s].wait_recv()
        if s == 0:
            continue
        line_out[s] = partial_ref[block((z + s) % line, y), :] + pair_in[s]
        line_copies[s] = pltpu.make_async_remote_copy(
            src_ref=line_out.at[s], dst_ref=line_in.at[s],
            send_sem=line_send.at[s], recv_sem=line_recv.at[s],
            device_id={"vir": ((z + s) % line) * 2 + y, "occ": occ},
            device_id_type=pl.DeviceIdType.MESH,
        )
        line_copies[s].start()
    total = partial_ref[block(z, y), :] + pair_in[0]
    for s in order[:-1]:
        line_copies[s].wait_recv()
        total = total + line_in[s]

    moved = jnp.dot(rows_out[...], total, precision=exact, preferred_element_type=jnp.float32)
    folded = jnp.zeros((half, lanes), jnp.float32)
    for fold in range(folds):
        folded = folded + jnp.dot(
            moved[fold * half:(fold + 1) * half], cols_out[fold],
            precision=exact, preferred_element_type=jnp.float32,
        )
    outgoing[...] = folded

    def cell(ref, v, o):
        return ref.at[
            pl.ds(pl.multiple_of(v * 8, 8), 8), pl.ds(pl.multiple_of(o * 128, 128), 128)
        ]

    def mirror_copy(k):
        other = (me + k) % devices
        v, o = other // occ_size, other % occ_size
        return pltpu.make_async_remote_copy(
            src_ref=cell(outgoing, v, o), dst_ref=cell(incoming, vir, occ),
            send_sem=mirror_send.at[k], recv_sem=mirror_recv.at[k],
            device_id={"vir": v, "occ": o},
            device_id_type=pl.DeviceIdType.MESH,
        )

    def send(k, carry):
        mirror_copy(k).start()
        return carry

    lax.fori_loop(1, devices, send, 0)
    cell(incoming, vir, occ)[...] = cell(outgoing, vir, occ)[...]

    def receive(k, carry):
        other = (me + devices - k) % devices
        v, o = other // occ_size, other % occ_size
        pltpu.make_async_remote_copy(
            src_ref=cell(outgoing, v, o), dst_ref=cell(incoming, v, o),
            send_sem=mirror_send.at[k], recv_sem=mirror_recv.at[k],
            device_id={"vir": v, "occ": o},
            device_id_type=pl.DeviceIdType.MESH,
        ).wait_recv()
        return carry

    lax.fori_loop(1, devices, receive, 0)
    unfolded = [
        jnp.dot(incoming[...], cols_in[fold], precision=exact, preferred_element_type=jnp.float32)
        for fold in range(folds)
    ]
    back = jnp.dot(
        rows_in[...], jnp.concatenate(unfolded, axis=0),
        precision=exact, preferred_element_type=jnp.float32,
    )
    out_ref[...] = total + back

    for s in order:
        pair_copies[s].wait_send()
        if s:
            line_copies[s].wait_send()

    def sent(k, carry):
        mirror_copy(k).wait_send()
        return carry

    lax.fori_loop(1, devices, sent, 0)


def exchange(partial_sum):
    vir_size, occ_size = lax.axis_size("vir"), lax.axis_size("occ")
    pair_rows, width = partial_sum.shape
    own_rows = pair_rows // vir_size
    line = vir_size // 2
    folds = 128 // (NO // occ_size) ** 2
    lanes = occ_size * 128
    block = (line, own_rows, width)
    devices = vir_size * occ_size
    return pl.pallas_call(
        functools.partial(exchange_kernel, vir_size, occ_size),
        out_shape=jax.ShapeDtypeStruct((own_rows, width), jnp.float32),
        in_specs=[pl.BlockSpec(memory_space=pltpu.VMEM)],
        out_specs=pl.BlockSpec(memory_space=pltpu.VMEM),
        scratch_shapes=[
            pltpu.VMEM(block, jnp.float32),
            pltpu.VMEM(block, jnp.float32),
            pltpu.VMEM(block, jnp.float32),
            pltpu.VMEM((vir_size * 8, lanes), jnp.float32),
            pltpu.VMEM((vir_size * 8, lanes), jnp.float32),
            pltpu.VMEM((own_rows, own_rows), jnp.float32),
            pltpu.VMEM((folds, width, lanes), jnp.float32),
            pltpu.VMEM((own_rows, own_rows), jnp.float32),
            pltpu.VMEM((folds, lanes, width), jnp.float32),
            pltpu.SemaphoreType.DMA((line,)),
            pltpu.SemaphoreType.DMA((line,)),
            pltpu.SemaphoreType.DMA((line,)),
            pltpu.SemaphoreType.DMA((line,)),
            pltpu.SemaphoreType.DMA((devices,)),
            pltpu.SemaphoreType.DMA((devices,)),
        ],
        compiler_params=pltpu.CompilerParams(
            collective_id=0, has_side_effects=True, vmem_limit_bytes=24 * MIB
        ),
    )(partial_sum)


def exchange_by_collectives(partial_sum):
    pair_rows, ij_dev = partial_sum.shape
    occ_local = ij_dev // NO
    swapped = partial_sum.reshape(NW, NW, ij_dev).transpose(1, 0, 2).reshape(pair_rows, ij_dev)
    moved = lax.all_to_all(
        swapped.reshape(pair_rows, occ_local, NO), "occ", split_axis=2, concat_axis=1, tiled=True
    )
    numerator = partial_sum + moved.transpose(0, 2, 1).reshape(pair_rows, ij_dev)
    return lax.psum_scatter(numerator, "vir", scatter_dimension=0, tiled=True)


def per_device(tiles, tile_slot, amplitudes, occ_energy, vir_energy):
    ij_dev = amplitudes.shape[1]
    pair_rows = NW * NW
    row_blocks = pair_rows // tiles.shape[1]
    own_rows = pair_rows // lax.axis_size("vir")
    row_ids = lax.axis_index("vir") * own_rows + jnp.arange(own_rows)
    orbital = jnp.arange(NW)
    picks = (row_ids[:, None] // NW == orbital[None, :], row_ids[:, None] % NW == orbital[None, :])
    vir_pair = sum(jnp.sum(jnp.where(p, vir_energy[None, :], 0.0), axis=1) for p in picks)
    col_ids = lax.axis_index("occ") * ij_dev + jnp.arange(ij_dev)
    occupied = jnp.arange(NO)
    picks = (col_ids[None, :] // NO == occupied[:, None], col_ids[None, :] % NO == occupied[:, None])
    occ_pair = sum(jnp.sum(jnp.where(p, occ_energy[:, None], 0.0), axis=0) for p in picks)
    partial_sum = ladder_partial(tiles, tile_slot, amplitudes, row_blocks)
    if mirror_fits(lax.axis_size("vir"), lax.axis_size("occ")):
        numerator = exchange(partial_sum)
    else:
        numerator = exchange_by_collectives(partial_sum)
    return numerator / (occ_pair[None, :] - vir_pair[:, None])


def solution(mesh):
    in_specs = (P("vir", None, None), P("vir"), P("vir", "occ"), P(), P())
    out_specs = P("vir", "occ")
    return jax.shard_map(
        per_device, mesh=mesh, in_specs=in_specs, out_specs=out_specs, check_vma=False
    )
```

time: 150 us -> 70.8 us (0.47); the launches traced: 149 us -> 71.8 us
  waiting for transfers between devices: 75.3 us -> 0 us
  Pallas kernels: 28.3 us -> 69.5 us
  blocking collectives: 18.5 us -> 0 us
  between operations: 13.5 us -> 0.06 us
  local copies, waits for them, and re-layouts: 9.38 us -> 1.23 us
  other arithmetic: 4.11 us -> 0.97 us
    reduce_scatter x1 -> x0, waiting for transfers between devices: 75.3 us -> none  [per_device(): total = lax.psum_scatter(numerator, 'vir', scatter_dimension=0, tiled=True)]
    pallas_call x0 -> x1, Pallas kernels: none -> 43.3 us  [exchange(): pl.pallas_call(functools.partial(exchange_kernel, vir_size, occ_size), ou...]
    all_to_all x1 -> x0, blocking collectives: 18.5 us -> none  [per_device(): lax.all_to_all(swapped.reshape(pair_rows, occ_local, NO), 'occ', split_ax...]
    another operation x2 -> x0, local copies, waits for them, and re-layouts: 5.65 us -> none  [per_device(): swapped.reshape(pair_rows, occ_local, NO)]
    add x2, other arithmetic: 2.34 us -> 0.01 us  [the longest x1 0.01 us: per_device(): sum((jnp.sum(jnp.where(p, vir_energy[None, :], 0.0), axis=1) for p in pic...]
    reshape x2 -> x0, local copies, waits for them, and re-layouts: 2.17 us -> none  [the longest x1 1.84 us: per_device(): partial_sum.reshape(NW, NW, ij_dev).transpose(1, 0, 2)]
    pallas_call x1, Pallas kernels: 28.3 us -> 26.2 us  [ladder_partial(): pl.pallas_call(functools.partial(ladder_kernel, row_blocks), out_shape=ja...]
  transfers between devices with their start and end apart: 1 -> 0, of which waited for: 1 -> 0; matrix products, arithmetic and copies ran while one was open for 0% -> 0% of each run, Pallas kernels for 0% -> 0%
where the time goes in v2:
time: 70.8 us; the launch traced here: 71.8 us
  Pallas kernels  69.5 us (98%)
  local copies, waits for them, and re-layouts  1.23 us (2%)
  other arithmetic  0.97 us (1%)
    pallas_call x1, Pallas kernels, exchange(): pl.pallas_call(functools.partial(exchange_kernel, vir_size, occ_size), ou...  43.3 us
    pallas_call x1, Pallas kernels, ladder_partial(): pl.pallas_call(functools.partial(ladder_kernel, row_blocks), out_shape=ja...  26.2 us

profile of v2, /device:TPU:0, one launch (start us, length us, event | category | flops | bytes accessed | tf_op | source)
XLA Modules:
  0.0 71.8 jit_solution(14432638512321416735)
XLA Ops:
  0.0 0.0 copy-start.1
  0.0 0.0 copy-start.2
  0.0 26.2 %shard_map.55.partial_ref = f32[1024,256]{1,0:T(8,128)} custom-call(s32[512]{0:T(512)} %slots_ref.1, s32[4,128]{1,0:T(4,128)} %bitcast.1, f32[512,128,128]{2,1,0:T(8,128)} %tiles_hbm.1, f32[32768,256]{1,0:T(8,128)} %amp_hbm.1), custom_call_target="tpu_custom_call" | custom-call | flops 12884901888 | bytes 67108864 | tf_op jit(solution)/shard_map/pallas_call | solution.py:138
  26.2 0.0 copy-start
  26.2 1.2 %copy-done = f32[1024,256]{1,0:T(8,128)S(1)} copy-done((f32[1024,256]{1,0:T(8,128)S(1)}, f32[1024,256]{1,0:T(8,128)}, u32[]{:S(2)}) %copy-start) | copy-done | bytes 1048600
  27.4 43.3 %shard_map.56 = f32[128,256]{1,0:T(8,128)S(1)} custom-call(f32[1024,256]{1,0:T(8,128)S(1)} %copy-done), custom_call_target="tpu_custom_call" | custom-call | tf_op jit(solution)/shard_map/pallas_call | solution.py:353
  70.8 0.0 copy-done.1
  70.8 0.1 select_reduce_fusion.2
  70.9 0.0 copy-done.2
  70.9 0.1 select_reduce_fusion
  71.0 0.8 %subtract_divide_fusion = f32[128,256]{1,0:T(8,128)} fusion(f32[128,256]{1,0:T(8,128)S(1)} %shard_map.56, f32[128]{0:T(128)S(1)} %add.81, f32[256]{0:T(256)S(1)} %add.77), kind=kLoop, calls=%fused_computation | loop fusion | flops 65536 | bytes 263680 | tf_op jit(solution)/shard_map/div | solution.py:410
  (4 shorter events, 0.0 us)
Async XLA Ops:
  0.0 70.8 %copy-start.1 = (f32[32]{0:T(128)S(1)}, f32[32]{0:T(128)}, u32[]{:S(2)}) copy-start(f32[32]{0:T(128)} %param.9) | copy-start | bytes 388
  0.0 70.9 %copy-start.2 = (f32[32]{0:T(128)S(1)}, f32[32]{0:T(128)}, u32[]{:S(2)}) copy-start(f32[32]{0:T(128)} %param.8) | copy-start | bytes 388
  26.2 1.2 %copy-start = (f32[1024,256]{1,0:T(8,128)S(1)}, f32[1024,256]{1,0:T(8,128)}, u32[]{:S(2)}) copy-start(f32[1024,256]{1,0:T(8,128)} %shard_map.55.partial_ref) | copy-start | bytes 3145732
